TPU v7x, 32 devices: a whole 2x2x4 slice. The times are simulated.
32 devices in a mesh: groups: 2 (over y), row: 8 (over z, x), col: 2 (over core).
Axes of the slice: x: 2, y: 2, z: 4, core: 2. Of those that a mesh axis runs over, the one named last changes fastest.
Arguments:
- acts: bfloat16 [2048, 8192], P(('groups', 'row'), 'col'), parts along dimension 0, may hold values from -6 to 6
- w_value: bfloat16 [8192, 1024], P('row', 'col'), may hold values from -0.0625 to 0.0625
- adapt_down: bfloat16 [8192, 64], P('row'), may hold values from -0.0625 to 0.0625
- adapter_up_factor: bfloat16 [64, 1024], P(None, 'col'), may hold values from -0.375 to 0.375
- cotangent: bfloat16 [2048, 1024], P(('groups', 'row'), 'col'), parts along dimension 0, may hold values from -6 to 6
Outputs:
- values: bfloat16 [2048, 1024], P(('groups', 'row'), 'col'), parts along dimension 0
- grad_acts: bfloat16 [2048, 8192], P(('groups', 'row'), 'col'), parts along dimension 0
- grad_down: float32 [16384, 64], P(('groups', 'row', 'col')), parts along dimension 0
- up_factor_gradient: float32 [128, 1024], P('groups', 'col'), parts along dimension 0
There are 2 independent parts, one for each index of `groups`. A program takes and returns all parts, laid end to end along the dimension named above; an argument that names none is the same for every part. Nothing has to cross between parts.
All inputs are finite; a program needn't handle non-finite values.
Results may differ from a plain program's by a relative error of at most 0.01.
Values may be sent and summed in bfloat16 or wider, within the bound.
A program may use at most 64 MiB of HBM per device.

v0:
```python
import math

import jax
import jax.numpy as jnp
from jax import lax
from jax.sharding import PartitionSpec as P

ADAPTER_SCALE = 2.0


def body(acts, w_value, adapt_down, adapter_up_factor, cotangent):
    whole = lax.all_gather(acts, "col", axis=1, tiled=True)
    tok_count = whole.shape[0]
    width = whole.shape[1]
    down_full = lax.all_gather(adapt_down, "row", axis=0, tiled=True)
    piece = lax.all_gather(w_value, "row", axis=0, tiled=True)
    span = whole
    base_output = jnp.dot(span, piece, preferred_element_type=jnp.float32)
    base_output, stored = (base_output, piece)
    low_sum = jnp.dot(whole, down_full, preferred_element_type=jnp.float32)
    low_rank_input = low_sum.astype(jnp.bfloat16)
    values = (
        base_output
        + ADAPTER_SCALE
        * jnp.dot(low_rank_input, adapter_up_factor, preferred_element_type=jnp.float32)
    ).astype(jnp.bfloat16)
    backward_piece = ADAPTER_SCALE * jnp.dot(
        cotangent, adapter_up_factor.T, preferred_element_type=jnp.float32
    )
    backward_result = lax.psum(backward_piece.astype(jnp.bfloat16), "col")
    total_tokens = tok_count * lax.axis_size("row")
    gradient_norm = 1.0 / math.sqrt(total_tokens)
    up_factor_piece = ADAPTER_SCALE * jnp.dot(
        low_rank_input.T, cotangent, preferred_element_type=jnp.float32
    )
    up_factor_gradient = lax.psum(up_factor_piece, "row") * gradient_norm
    col_index = lax.axis_index("col")
    pair_count = lax.axis_size("col")
    tok_half = tok_count // pair_count
    mine_acts = lax.dynamic_slice_in_dim(whole, col_index * tok_half, tok_half, 0)
    mine_back = lax.dynamic_slice_in_dim(backward_result, col_index * tok_half, tok_half, 0)
    span = mine_acts
    grad_down = (
        lax.psum_scatter(
            jnp.dot(span.T, mine_back, preferred_element_type=jnp.float32),
            ("row", "col"),
            scatter_dimension=0,
            tiled=True,
        )
        * gradient_norm
    )
    d_half = width // pair_count
    down_mine = lax.dynamic_slice_in_dim(down_full, col_index * d_half, d_half, 0)
    adapter_dx = jnp.dot(backward_result, down_mine.T, preferred_element_type=jnp.float32)
    partial_dx = jnp.dot(cotangent, stored.T, preferred_element_type=jnp.float32)
    base_dx = lax.psum_scatter(
        partial_dx.astype(jnp.bfloat16), "col", scatter_dimension=1, tiled=True
    ).astype(jnp.float32)
    grad_acts = (base_dx + adapter_dx).astype(jnp.bfloat16)
    return (values, grad_acts, grad_down, up_factor_gradient)


def solution(mesh):
    return jax.shard_map(
        body,
        mesh=mesh,
        in_specs=(
            P(("groups", "row"), "col"),
            P("row", "col"),
            P("row", None),
            P(None, "col"),
            P(("groups", "row"), "col"),
        ),
        out_specs=(
            P(("groups", "row"), "col"),
            P(("groups", "row"), "col"),
            P(("groups", "row", "col"), None),
            P("groups", "col"),
        ),
        check_vma=False,
    )
```

profile of v0, /device:TPU:0, one launch (start us, length us, event | category | flops | bytes accessed | tf_op | source)
XLA Modules:
  0.0 349.2 jit_solution(4356714957952916571)
XLA Ops:
  7.2 0.7 all-gather.8.cloned.1.call-update
  7.9 0.0 all-gather.4.cloned.1.call-start
  8.0 0.7 all-gather.4.cloned.1.call-update
  8.7 0.7 all-gather.6.cloned.1.call-update
  9.4 0.0 all-reduce.2.cloned.1.call-start
  9.5 0.2 fusion.3
  9.6 3.6 %psum.14 = bf16[128,64]{0,1:T(8,128)(2,1)S(1)} all-reduce(bf16[128,64]{0,1:T(8,128)(2,1)S(1)} %fusion.3), channel_id=1, replica_groups=mesh['groups'=2,'row'=8,'col'=2] {'col'}, use_global_device_ids=true, to_apply=%region_1.0 | all-reduce | flops 8192 | bytes 32768 | tf_op jit(solution)/shard_map/psum | solution.py:30
  13.3 39.8 %all-gather.8.cloned.1.call-done = bf16[8192,64]{0,1:T(8,128)(2,1)} async-done(((bf16[1024,64]{0,1:T(8,128)(2,1)}), bf16[8192,64]{0,1:T(8,128)(2,1)}) %all-gather.8.cloned.1.call-update) | async-done | bytes 1048592 | tf_op jit(solution)/shard_map/all_gather | solution.py:15
  53.1 10.9 %all-gather.4.cloned.1.call-done = bf16[128,8192]{1,0:T(8,128)(2,1)} async-done(((bf16[128,4096]{1,0:T(8,128)(2,1)}), bf16[128,8192]{1,0:T(8,128)(2,1)}) %all-gather.4.cloned.1.call-update) | async-done | bytes 2097168 | tf_op jit(solution)/shard_map/all_gather | solution.py:12
  64.0 2.8 convolution_convert_fusion.1
  66.9 0.8 convolution_multiply_fusion.1
  67.7 0.0 reduce-scatter.5.cloned.1.call-start
  67.8 1.8 fusion.4
  69.6 0.0 reduce-scatter.3.cloned.1.call-start
  69.7 122.6 %all-gather.6.cloned.1.call-done = bf16[8192,512]{1,0:T(8,128)(2,1)} async-done(((bf16[1024,512]{1,0:T(8,128)(2,1)}), bf16[8192,512]{1,0:T(8,128)(2,1)}) %all-gather.6.cloned.1.call-update) | async-done | bytes 8388624 | tf_op jit(solution)/shard_map/all_gather | solution.py:16
  192.3 7.5 %convolution_convert_fusion = bf16[128,8192]{1,0:T(8,128)(2,1)} fusion(bf16[128,512]{1,0:T(8,128)(2,1)S(1)} %copy-done, bf16[8192,512]{1,0:T(8,128)(2,1)} %all-gather.6.cloned.1.call-done), kind=kOutput, calls=%fused_computation | convolution fusion | flops 1074790400 | bytes 10616832 | tf_op jit(solution)/shard_map/dot_general | solution.py:55
  199.9 64.2 %all-reduce.2.cloned.1.call-done = f32[64,512]{1,0:T(8,128)} async-done(((f32[64,512]{1,0:T(8,128)}), f32[64,512]{1,0:T(8,128)}) %all-reduce.2.cloned.1.call-update) | async-done | bytes 131088 | tf_op jit(solution)/shard_map/psum | solution.py:36
  264.0 1.6 broadcast_multiply_fusion
  265.6 63.3 %reduce-scatter.5.cloned.1.call-done = f32[512,64]{0,1:T(8,128)} async-done(((f32[8192,64]{0,1:T(8,128)}), f32[512,64]{0,1:T(8,128)}) %reduce-scatter.5.cloned.1.call-update) | async-done | bytes 131088 | tf_op jit(solution)/shard_map/reduce_scatter | solution.py:44
  328.9 1.6 broadcast_multiply_fusion.1
  330.5 4.7 %fusion.10 = f32[128,512]{1,0:T(8,128)S(1)} fusion(bf16[128,8192]{1,0:T(8,128)(2,1)S(1)} %copy-done.1, bf16[8192,512]{1,0:T(8,128)(2,1)} %all-gather.6.cloned.1.call-done), kind=kOutput, calls=%fused_computation.18 | convolution fusion | flops 1073741824 | bytes 10747904 | tf_op jit(solution)/shard_map/dot_general | solution.py:18
  335.2 0.9 fusion.2
  336.1 3.6 %reduce-scatter.3.cloned.1.call-done = bf16[128,4096]{1,0:T(8,128)(2,1)} async-done(((bf16[128,8192]{1,0:T(8,128)(2,1)}), bf16[128,4096]{1,0:T(8,128)(2,1)}) %reduce-scatter.3.cloned.1.call-update) | async-done | bytes 1048592 | tf_op jit(solution)/shard_map/reduce_scatter | solution.py:56
  339.7 2.6 fusion
  (13 shorter events, 0.1 us)
Async XLA Ops:
  7.2 2.3 copy-start
  7.2 2.3 copy-start.3
  7.2 45.9 %all-gather.8.cloned.1.call-start = ((), (), s32[]{:S(2)}) async-start(), calls=%async_computation.4 | async-start | bytes 1179648 | tf_op jit(solution)/shard_map/all_gather | solution.py:15
  7.9 56.1 %all-gather.4.cloned.1.call-start = ((), (), s32[]{:S(2)}) async-start(), calls=%async_computation.2 | async-start | bytes 3145728 | tf_op jit(solution)/shard_map/all_gather | solution.py:12
  8.7 183.6 %all-gather.6.cloned.1.call-start = ((), (), s32[]{:S(2)}) async-start(), calls=%async_computation.3 | async-start | bytes 9437184 | tf_op jit(solution)/shard_map/all_gather | solution.py:16
  9.4 254.6 %all-reduce.2.cloned.1.call-start = ((), (), s32[]{:S(2)}) async-start(), calls=%async_computation.7 | async-start | bytes 262144 | tf_op jit(solution)/shard_map/psum | solution.py:36
  64.0 3.7 %copy-start.1 = (bf16[128,8192]{1,0:T(8,128)(2,1)S(1)}, bf16[128,8192]{1,0:T(8,128)(2,1)}, u32[]{:S(2)}) copy-start(bf16[128,8192]{1,0:T(8,128)(2,1)} %all-gather.4.cloned.1.call-done) | copy-start | bytes 6291460
  67.7 261.2 %reduce-scatter.5.cloned.1.call-start = ((), (), s32[]{:S(2)}) async-start(), calls=%async_computation.6 | async-start | bytes 2228224 | tf_op jit(solution)/shard_map/reduce_scatter | solution.py:44
  69.6 270.1 %reduce-scatter.3.cloned.1.call-start = ((), (), s32[]{:S(2)}) async-start(), calls=%async_computation.5 | async-start | bytes 3145728 | tf_op jit(solution)/shard_map/reduce_scatter | solution.py:56
  330.5 9.2 %copy-start.2 = (bf16[8192,64]{0,1:T(8,128)(2,1)S(1)}, bf16[8192,64]{0,1:T(8,128)(2,1)}, u32[]{:S(2)}) copy-start(bf16[8192,64]{0,1:T(8,128)(2,1)} %all-gather.8.cloned.1.call-done) | copy-start | bytes 3145732
Sparse Core Ops, SparseCore 0:
  10.2 42.8 all-gather.7
  54.7 9.3 all-gather.3
  66.2 126.0 all-gather.5
  196.1 67.8 all-reduce.1
  268.1 60.8 reduce-scatter.4
  331.0 8.6 reduce-scatter.2
where the time goes:
time: 349 us
  waiting for transfers between devices  307 us (88%)
  matrix products  21.4 us (6%)
  between operations  14.2 us (4%)
  blocking collectives  3.65 us (1%)
    all_gather x1, waiting for transfers between devices, body(): piece = lax.all_gather(w_value, 'row', axis=0, tiled=True)  123 us
    psum x1, waiting for transfers between devices, body(): up_factor_gradient = lax.psum(up_factor_piece, 'row') * gradient_norm  64.2 us
    reduce_scatter x1, waiting for transfers between devices, body(): lax.psum_scatter(jnp.dot(span.T, mine_back, preferred_element_type=jnp.fl...  63.3 us
    all_gather x1, waiting for transfers between devices, body(): down_full = lax.all_gather(adapt_down, 'row', axis=0, tiled=True)  39.8 us
    all_gather x1, waiting for transfers between devices, body(): whole = lax.all_gather(acts, 'col', axis=1, tiled=True)  10.9 us
    dot_general x1, matrix products, body(): jnp.dot(cotangent, stored.T, preferred_element_type=jnp.float32)  7.55 us
  transfers between devices with their start and end apart: 6, of which 6 were waited for; matrix products, arithmetic and copies ran while one was open for 6% of the time, Pallas kernels for 0%

commit v1 on v0

--- a/solution.py
+++ b/solution.py
@@ -1,11 +1,402 @@
+import functools
 import math
 
 import jax
 import jax.numpy as jnp
 from jax import lax
+from jax.experimental import pallas as pl
+from jax.experimental.pallas import tpu as pltpu
 from jax.sharding import PartitionSpec as P
 
 ADAPTER_SCALE = 2.0
+MESH = pl.DeviceIdType.MESH
+F32 = jnp.float32
+BF16 = jnp.bfloat16
+
+
+def dot(a, b, da=1, db=0):
+    return lax.dot_general(a, b, (((da,), (db,)), ((), ())), preferred_element_type=F32)
+
+
+def exchange_kernel(
+    nz,
+    norm,
+    acts,
+    w,
+    down_t,
+    up,
+    cot,
+    values,
+    gacts,
+    gdown,
+    gup,
+    xa,
+    ct,
+    uf,
+    df,
+    wf,
+    gds,
+    gdr,
+    lows,
+    lowr,
+    ups,
+    upx,
+    upz,
+    upd,
+    gas,
+    vs,
+    vr,
+    vacc,
+    s_acts,
+    r_acts,
+    s_cot,
+    r_cot,
+    s_up,
+    r_up,
+    s_dn,
+    r_dn,
+    s_w,
+    r_w,
+    s_wl,
+    r_wl,
+    s_f,
+    r_f,
+    s_gd,
+    r_gd,
+    s_low,
+    r_low,
+    s_ux,
+    r_ux,
+    s_uz,
+    r_uz,
+    s_ud,
+    r_ud,
+    s_ga,
+    r_ga,
+    s_v,
+    r_v,
+):
+    y, row, c = lax.axis_index("groups"), lax.axis_index("row"), lax.axis_index("col")
+    z, x = row // 2, row % 2
+    tok, depth, feat = acts.shape[0], w.shape[0], w.shape[1]
+    rank = up.shape[0]
+    half, hr = depth // 2, rank // 2
+    blocks = nz // 2
+    home, place = z // blocks, z % blocks
+    xo, co, yo = 1 - x, 1 - c, 1 - y
+
+    def dev(yy, zz, xx, cc):
+        return (yy, zz * 2 + xx, cc)
+
+    def cols(i, n):
+        return pl.ds(pl.multiple_of(i * n, n), n)
+
+    def rc(src, dst, ss, rs, to):
+        return pltpu.make_async_remote_copy(
+            src_ref=src, dst_ref=dst, send_sem=ss, recv_sem=rs, device_id=to, device_id_type=MESH
+        )
+
+    other = dev(y, z, xo, c)
+
+    def arrived(dst, rs):
+        rc(dst, dst, rs, rs, other).wait_recv()
+
+    mates = [(x, co), (xo, c), (xo, co)]
+    zs = [lax.rem(z + k, nz) for k in range(1, nz)]
+
+    barrier = pltpu.get_barrier_semaphore()
+    peers = [dev(y, z, a, b) for a, b in mates] + [dev(yo, z, x, c)]
+    peers += [dev(y, t, x, b) for t in zs for b in range(2)]
+    for p in peers:
+        pl.semaphore_signal(barrier, inc=1, device_id=p, device_id_type=MESH)
+    pl.semaphore_wait(barrier, len(peers))
+
+    sent = []
+
+    mine = (cols(x, tok), cols(c, feat))
+    for i, (a, b) in enumerate(mates):
+        cp = rc(cot, ct.at[mine], s_cot.at[i], r_cot.at[x * 2 + c], dev(y, z, a, b))
+        cp.start()
+        sent.append(cp)
+    cp = rc(up, uf.at[:, cols(c, feat)], s_up, r_up, dev(y, z, x, co))
+    cp.start()
+    sent.append(cp)
+    for b in range(blocks):
+        cp = rc(
+            acts.at[:, cols(b * 2 + xo, depth)],
+            xa.at[b, cols(x, tok), :],
+            s_acts.at[b],
+            r_acts.at[b],
+            other,
+        )
+        cp.start()
+        sent.append(cp)
+
+    dn_copies = [
+        rc(down_t, df.at[place], s_dn.at[k], r_dn.at[place], dev(y, t, x, c))
+        for k, t in enumerate(zs)
+    ]
+
+    @pl.when(c == home)
+    def _():
+        for cp in dn_copies:
+            cp.start()
+
+    w_local = rc(w, wf.at[place, :, cols(c, feat)], s_wl, r_wl, dev(y, z, x, co))
+
+    for k, t in enumerate(zs):
+        cp = rc(
+            w.at[cols(y, half), :],
+            wf.at[place, cols(y, half), cols(c, feat)],
+            s_w.at[k],
+            r_w.at[place, c],
+            dev(y, t, x, home),
+        )
+        cp.start()
+        sent.append(cp)
+
+    @pl.when(c != home)
+    def _():
+        w_local.start()
+
+    ct[mine] = cot[...]
+    uf[:, cols(c, feat)] = up[...]
+    for b in range(blocks):
+        xa[b, cols(x, tok), :] = acts[:, cols(b * 2 + x, depth)]
+
+    @pl.when(c == home)
+    def _():
+        df[place] = down_t[...]
+        wf[place, :, cols(c, feat)] = w[...]
+
+    for a, b in mates:
+        arrived(ct.at[cols(a, tok), cols(b, feat)], r_cot.at[a * 2 + b])
+    arrived(uf.at[:, cols(co, feat)], r_up)
+    back = (ADAPTER_SCALE * dot(ct[...], uf[...], 1, 1)).astype(BF16)
+    gd_copies = []
+    for b in range(blocks):
+        arrived(xa.at[b, cols(xo, tok), :], r_acts.at[b])
+        gds[b] = dot(back, xa[b], 0, 0)
+        t = c * blocks + b
+        for e in range(2):
+            cp = rc(
+                gds.at[b, :, pl.ds(e * half, half)],
+                gdr.at[z],
+                s_gd.at[b, e],
+                r_gd.at[z],
+                dev(y, t, x, e),
+            )
+            here = (t == z) & (c == e)
+            gd_copies.append((here, cp))
+
+            @pl.when(here)
+            def _():
+                gdr[z] = gds[b, :, e * half : (e + 1) * half]
+
+            @pl.when(jnp.logical_not(here))
+            def _():
+                cp.start()
+
+    low_t = jnp.zeros((rank, 2 * tok), F32)
+    for b in range(blocks):
+
+        @pl.when(c * blocks + b != z)
+        def _():
+            arrived(df.at[b], r_dn.at[b])
+
+        low_t += dot(df[b], xa[b], 1, 1)
+    lows[0] = low_t[:, :tok]
+    lows[1] = low_t[:, tok:]
+    for i, (a, b) in enumerate(mates):
+        cp = rc(lows.at[a], lowr.at[x * 2 + c], s_low.at[i], r_low.at[x * 2 + c], dev(y, z, a, b))
+        cp.start()
+        sent.append(cp)
+    low = lows[x]
+    for a, b in mates:
+        arrived(lowr.at[a * 2 + b], r_low.at[a * 2 + b])
+        low += lowr[a * 2 + b]
+    low = low.astype(BF16)
+
+    ups[...] = ADAPTER_SCALE * dot(low, ct[mine])
+    cp = rc(ups.at[cols(xo, hr), :], upx, s_ux, r_ux, other)
+    cp.start()
+    sent.append(cp)
+    arrived(upx, r_ux)
+    upz[z] = ups[cols(x, hr), :] + upx[...]
+    for k, t in enumerate(zs):
+        cp = rc(upz.at[z], upz.at[z], s_uz.at[k], r_uz.at[z], dev(y, t, x, c))
+        cp.start()
+        sent.append(cp)
+
+    order = [lax.rem(place + b, blocks) for b in range(blocks)]
+    forwards = []
+    for b in order:
+        absent = c * blocks + b != z
+        for e in range(2):
+            piece = wf.at[b, cols(y, half), pl.ds(e * feat, feat)]
+            cp = rc(piece, piece, s_f.at[b, e], r_f.at[b, e], dev(yo, z, x, c))
+            forwards.append((absent, cp))
+
+            @pl.when(absent)
+            def _():
+                arrived(piece, r_w.at[b, e])
+                cp.start()
+
+    for t in zs:
+        arrived(upz.at[t], r_uz.at[t])
+    total = upz[0]
+    for t in range(1, nz):
+        total += upz[t]
+    upd[...] = total * norm
+    gup[cols(x, hr), :] = upd[...]
+    cp = rc(upd, gup.at[cols(x, hr), :], s_ud, r_ud, other)
+    cp.start()
+    sent.append(cp)
+
+    for t in zs:
+        arrived(gdr.at[t], r_gd.at[t])
+
+    @pl.when(c != home)
+    def _():
+        arrived(gdr.at[z], r_gd.at[z])
+
+    total = gdr[0]
+    for t in range(1, nz):
+        total += gdr[t]
+    gdown[...] = (total * norm).T
+
+    for i, b in enumerate(order):
+        absent = c * blocks + b != z
+
+        @pl.when(absent)
+        def _():
+            for e in range(2):
+                arrived(wf.at[b, cols(yo, half), pl.ds(e * feat, feat)], r_f.at[b, e])
+
+        @pl.when(jnp.logical_not(absent))
+        def _():
+            arrived(wf.at[b, :, cols(co, feat)], r_wl)
+
+        grad = dot(back, df[b])
+        for e in range(2):
+            part = dot(ct[:, e * feat : (e + 1) * feat], wf[b, :, e * feat : (e + 1) * feat], 1, 1)
+            grad += part.astype(BF16).astype(F32)
+        gas[i] = grad.astype(BF16)
+        block = cols(b * 2 + x, depth)
+        cp = rc(
+            gas.at[i, cols(xo, tok), :], gacts.at[:, block], s_ga.at[b], r_ga.at[b], other
+        )
+        cp.start()
+        sent.append(cp)
+        part = dot(xa[b], wf[b])
+        if i == 0:
+            vacc[...] = part
+        else:
+            vacc[...] += part
+        gacts[:, block] = gas[i, cols(x, tok), :]
+
+    vs[...] = vacc[...].astype(BF16)
+    for i, (a, b) in enumerate(mates):
+        cp = rc(
+            vs.at[cols(a, tok), cols(b, feat)],
+            vr.at[x * 2 + c],
+            s_v.at[i],
+            r_v.at[x * 2 + c],
+            dev(y, z, a, b),
+        )
+        cp.start()
+        sent.append(cp)
+    out = vacc[mine] + ADAPTER_SCALE * dot(low, up[...], 0, 0)
+    for a, b in mates:
+        arrived(vr.at[a * 2 + b], r_v.at[a * 2 + b])
+        out += vr[a * 2 + b].astype(F32)
+    values[...] = out.astype(BF16)
+
+    arrived(gup.at[cols(xo, hr), :], r_ud)
+    for b in range(blocks):
+        arrived(gacts.at[:, cols(b * 2 + xo, depth)], r_ga.at[b])
+    for cp in sent:
+        cp.wait_send()
+    for here, cp in gd_copies:
+
+        @pl.when(jnp.logical_not(here))
+        def _():
+            cp.wait_send()
+
+    for absent, cp in forwards:
+
+        @pl.when(absent)
+        def _():
+            cp.wait_send()
+
+    @pl.when(c == home)
+    def _():
+        for cp in dn_copies:
+            cp.wait_send()
+
+    @pl.when(c != home)
+    def _():
+        w_local.wait_send()
+
+
+def kernel_body(acts, w_value, adapt_down, adapter_up_factor, cotangent):
+    tok, width = acts.shape
+    depth, feat = w_value.shape
+    rank = adapter_up_factor.shape[0]
+    rows = lax.axis_size("row")
+    nz = rows // 2
+    blocks, half, hr = nz // 2, depth // 2, rank // 2
+    norm = 1.0 / math.sqrt(tok * rows)
+    vmem = pl.BlockSpec(memory_space=pltpu.VMEM)
+    dma = lambda *s: pltpu.SemaphoreType.DMA(s) if s else pltpu.SemaphoreType.DMA
+    scratch = [
+        pltpu.VMEM((blocks, 2 * tok, depth), BF16),
+        pltpu.VMEM((2 * tok, 2 * feat), BF16),
+        pltpu.VMEM((rank, 2 * feat), BF16),
+        pltpu.VMEM((blocks, rank, depth), BF16),
+        pltpu.VMEM((blocks, depth, 2 * feat), BF16),
+        pltpu.VMEM((blocks, rank, depth), F32),
+        pltpu.VMEM((nz, rank, half), F32),
+        pltpu.VMEM((2, rank, tok), F32),
+        pltpu.VMEM((4, rank, tok), F32),
+        pltpu.VMEM((rank, feat), F32),
+        pltpu.VMEM((hr, feat), F32),
+        pltpu.VMEM((nz, hr, feat), F32),
+        pltpu.VMEM((hr, feat), F32),
+        pltpu.VMEM((blocks, 2 * tok, depth), BF16),
+        pltpu.VMEM((2 * tok, 2 * feat), BF16),
+        pltpu.VMEM((4, tok, feat), BF16),
+        pltpu.VMEM((2 * tok, 2 * feat), F32),
+        dma(blocks), dma(blocks),
+        dma(3), dma(4),
+        dma(), dma(),
+        dma(nz - 1), dma(blocks),
+        dma(nz - 1), dma(blocks, 2),
+        dma(), dma(),
+        dma(blocks, 2), dma(blocks, 2),
+        dma(blocks, 2), dma(nz),
+        dma(3), dma(4),
+        dma(), dma(),
+        dma(nz - 1), dma(nz),
+        dma(), dma(),
+        dma(blocks), dma(blocks),
+        dma(3), dma(4),
+    ]
+    return pl.pallas_call(
+        functools.partial(exchange_kernel, nz, norm),
+        out_shape=(
+            jax.ShapeDtypeStruct((tok, feat), BF16),
+            jax.ShapeDtypeStruct((tok, width), BF16),
+            jax.ShapeDtypeStruct((half, rank), F32),
+            jax.ShapeDtypeStruct((rank, feat), F32),
+        ),
+        in_specs=[vmem] * 5,
+        out_specs=(vmem,) * 4,
+        scratch_shapes=scratch,
+        compiler_params=pltpu.CompilerParams(
+            collective_id=0, has_side_effects=True, vmem_limit_bytes=48 * 2**20
+        ),
+    )(acts, w_value, adapt_down.T, adapter_up_factor, cotangent)
 
 
 def body(acts, w_value, adapt_down, adapter_up_factor, cotangent):
@@ -60,9 +451,16 @@
     return (values, grad_acts, grad_down, up_factor_gradient)
 
 
+def pick(mesh, *arrays):
+    rows, tiles = lax.axis_size("row"), arrays[1].shape[0] % 256 == 0
+    fits = rows % 4 == 0 and mesh.shape["groups"] == 2 and mesh.shape["col"] == 2
+    step = kernel_body if fits and tiles else body
+    return step(*arrays)
+
+
 def solution(mesh):
     return jax.shard_map(
-        body,
+        functools.partial(pick, mesh),
         mesh=mesh,
         in_specs=(
             P(("groups", "row"), "col"),

time: 349 us -> 111 us (0.32)
  the two profiles are of different devices: /device:TPU:0 before, /device:TPU:25 now
where the time goes in v1:
time: 111 us
  Pallas kernels  102 us (92%)
  local copies, waits for them, and re-layouts  8.14 us (7%)
    pallas_call x1, Pallas kernels, kernel_body(): pl.pallas_call(functools.partial(exchange_kernel, nz, norm), out_shape=(j...  102 us
    unnamed x13, local copies, waits for them, and re-layouts  7.37 us

profile of v1, /device:TPU:25, one launch (start us, length us, event | category | flops | bytes accessed | tf_op | source)
XLA Modules:
  0.0 110.8 jit_solution(10240662752542885467)
XLA Ops:
  0.6 0.0 copy-start
  0.6 1.2 %copy-done = bf16[128,4096]{1,0:T(8,128)(2,1)S(1)} copy-done((bf16[128,4096]{1,0:T(8,128)(2,1)S(1)}, bf16[128,4096]{1,0:T(8,128)(2,1)}, u32[]{:S(2)}) %copy-start) | copy-done | bytes 1048600
  1.9 0.0 copy-start.1
  1.9 1.2 %copy-done.1 = bf16[1024,512]{1,0:T(8,128)(2,1)S(1)} copy-done((bf16[1024,512]{1,0:T(8,128)(2,1)S(1)}, bf16[1024,512]{1,0:T(8,128)(2,1)}, u32[]{:S(2)}) %copy-start.1) | copy-done | bytes 1048600
  3.1 0.0 copy-start.2
  3.1 0.9 copy-done.2
  4.0 0.0 copy-start.3
  4.0 0.9 copy-done.3
  4.9 0.0 copy-start.4
  4.9 0.8 copy-done.4
  5.7 102.0 %shard_map.84 = (bf16[128,512]{1,0:T(8,128)(2,1)S(1)}, bf16[128,4096]{1,0:T(8,128)(2,1)S(1)}, f32[512,64]{1,0:T(8,128)S(1)}, f32[64,512]{1,0:T(8,128)S(1)}) custom-call(bf16[128,4096]{1,0:T(8,128)(2,1)S(1)} %copy-done, bf16[1024,512]{1,0:T(8,128)(2,1)S(1)} %copy-done.1, bf16[64,1024]{1,0:T(8,128)(2,1)S(1)} %bitcast.1, bf16[64,512]{1,0:T(8,128)(2,1)S(1)} %copy-done.4, ...), custom_call_target="tpu_custom_call" | custom-call | tf_op jit(solution)/shard_map/pallas_call | solution.py:385
  107.7 0.8 copy.9
  108.5 0.7 copy.13
  109.1 1.0 copy.14
  110.1 0.7 copy.15
Async XLA Ops:
  0.6 1.2 %copy-start = (bf16[128,4096]{1,0:T(8,128)(2,1)S(1)}, bf16[128,4096]{1,0:T(8,128)(2,1)}, u32[]{:S(2)}) copy-start(bf16[128,4096]{1,0:T(8,128)(2,1)} %acts.1) | copy-start | bytes 3145732
  1.9 1.2 %copy-start.1 = (bf16[1024,512]{1,0:T(8,128)(2,1)S(1)}, bf16[1024,512]{1,0:T(8,128)(2,1)}, u32[]{:S(2)}) copy-start(bf16[1024,512]{1,0:T(8,128)(2,1)} %w.1) | copy-start | bytes 3145732
  3.1 0.9 copy-start.2
  4.0 0.9 copy-start.3
  4.9 0.8 copy-start.4

commit v2 on v1

--- a/solution.py
+++ b/solution.py
@@ -10,6 +10,7 @@
 
 ADAPTER_SCALE = 2.0
 MESH = pl.DeviceIdType.MESH
+PIECES = 2
 F32 = jnp.float32
 BF16 = jnp.bfloat16
 
@@ -61,6 +62,8 @@
     r_wl,
     s_f,
     r_f,
+    s_h,
+    s_in,
     s_gd,
     r_gd,
     s_low,
@@ -81,6 +84,7 @@
     tok, depth, feat = acts.shape[0], w.shape[0], w.shape[1]
     rank = up.shape[0]
     half, hr = depth // 2, rank // 2
+    rows = half // PIECES
     blocks = nz // 2
     home, place = z // blocks, z % blocks
     xo, co, yo = 1 - x, 1 - c, 1 - y
@@ -144,30 +148,97 @@
 
     w_local = rc(w, wf.at[place, :, cols(c, feat)], s_wl, r_wl, dev(y, z, x, co))
 
-    for k, t in enumerate(zs):
-        cp = rc(
-            w.at[cols(y, half), :],
-            wf.at[place, cols(y, half), cols(c, feat)],
-            s_w.at[k],
-            r_w.at[place, c],
-            dev(y, t, x, home),
+    own_sends = []
+    for i, t in enumerate((z + 1, z - 1)):
+        there = (t >= 0) & (t < nz)
+        for q in range(PIECES):
+            piece = cols(y * PIECES + q, rows)
+            cp = rc(
+                w.at[piece, :],
+                wf.at[place, piece, cols(c, feat)],
+                s_w.at[i, q],
+                r_w.at[place, c, q],
+                dev(y, jnp.clip(t, 0, nz - 1), x, home),
+            )
+            own_sends.append((there, cp))
+
+            @pl.when(there)
+            def _():
+                cp.start()
+
+    @pl.when(c != home)
+    def _():
+        w_local.start()
+
+    into = [
+        pltpu.make_async_copy(cot, ct.at[mine], s_in.at[0]),
+        pltpu.make_async_copy(up, uf.at[:, cols(c, feat)], s_in.at[1]),
+    ]
+    for b in range(blocks):
+        into.append(
+            pltpu.make_async_copy(
+                acts.at[:, cols(b * 2 + x, depth)], xa.at[b, cols(x, tok), :], s_in.at[4 + b]
+            )
         )
+    into_home = [
+        pltpu.make_async_copy(down_t, df.at[place], s_in.at[2]),
+        pltpu.make_async_copy(w, wf.at[place, :, cols(c, feat)], s_in.at[3]),
+    ]
+    for cp in into:
         cp.start()
-        sent.append(cp)
-
-    @pl.when(c != home)
-    def _():
-        w_local.start()
-
-    ct[mine] = cot[...]
-    uf[:, cols(c, feat)] = up[...]
-    for b in range(blocks):
-        xa[b, cols(x, tok), :] = acts[:, cols(b * 2 + x, depth)]
 
     @pl.when(c == home)
     def _():
-        df[place] = down_t[...]
-        wf[place, :, cols(c, feat)] = w[...]
+        for cp in into_home:
+            cp.start()
+
+    def in_order(i, first):
+        return jnp.where(
+            c == home, lax.rem(place + first + i, blocks), jnp.where(c > home, i, blocks - 1 - i)
+        )
+
+    forwards = []
+
+    def pass_on(b):
+        source = c * blocks + b
+        absent = source != z
+        t = jnp.where(source < z, z + 1, z - 1)
+        more = absent & (t >= 0) & (t < nz)
+        for q in range(PIECES):
+            for e in range(2):
+                piece = wf.at[b, cols(y * PIECES + q, rows), pl.ds(e * feat, feat)]
+                hop = rc(
+                    piece,
+                    piece,
+                    s_h.at[b, e, q],
+                    r_w.at[b, e, q],
+                    dev(y, jnp.clip(t, 0, nz - 1), x, c),
+                )
+                side = rc(piece, piece, s_f.at[b, e, q], r_f.at[b, e, q], dev(yo, z, x, c))
+                forwards.append((more, hop))
+                forwards.append((absent, side))
+
+                @pl.when(absent)
+                def _():
+                    arrived(piece, r_w.at[b, e, q])
+
+                @pl.when(more)
+                def _():
+                    hop.start()
+
+                @pl.when(absent)
+                def _():
+                    side.start()
+
+    pass_on(in_order(0, 1))
+
+    for cp in into:
+        cp.wait()
+
+    @pl.when(c == home)
+    def _():
+        for cp in into_home:
+            cp.wait()
 
     for a, b in mates:
         arrived(ct.at[cols(a, tok), cols(b, feat)], r_cot.at[a * 2 + b])
@@ -176,7 +247,7 @@
     gd_copies = []
     for b in range(blocks):
         arrived(xa.at[b, cols(xo, tok), :], r_acts.at[b])
-        gds[b] = dot(back, xa[b], 0, 0)
+        gds[b] = dot(back, xa[b], 0, 0).astype(BF16)
         t = c * blocks + b
         for e in range(2):
             cp = rc(
@@ -211,6 +282,52 @@
         cp = rc(lows.at[a], lowr.at[x * 2 + c], s_low.at[i], r_low.at[x * 2 + c], dev(y, z, a, b))
         cp.start()
         sent.append(cp)
+    def work_on(b, first):
+        absent = c * blocks + b != z
+
+        @pl.when(jnp.logical_not(absent))
+        def _():
+            arrived(wf.at[b, :, cols(co, feat)], r_wl)
+
+        for q in range(PIECES):
+            for h in (y, yo):
+                chunk = cols(h * PIECES + q, rows)
+                if h is yo:
+
+                    @pl.when(absent)
+                    def _():
+                        for e in range(2):
+                            arrived(wf.at[b, chunk, pl.ds(e * feat, feat)], r_f.at[b, e, q])
+
+                part = dot(xa[b, :, chunk], wf[b, chunk, :])
+                if first and q == 0 and h is y:
+                    vacc[...] = part
+                else:
+                    vacc[...] += part
+                grad = dot(back, df[b, :, chunk])
+                for e in range(2):
+                    part = dot(
+                        ct[:, e * feat : (e + 1) * feat],
+                        wf[b, chunk, e * feat : (e + 1) * feat],
+                        1,
+                        1,
+                    )
+                    grad += part.astype(BF16).astype(F32)
+                gas[b, :, chunk] = grad.astype(BF16)
+                place_of = cols(((b * 2 + x) * 2 + h) * PIECES + q, rows)
+                cp = rc(
+                    gas.at[b, cols(xo, tok), chunk],
+                    gacts.at[:, place_of],
+                    s_ga.at[b, h, q],
+                    r_ga.at[b, h, q],
+                    other,
+                )
+                cp.start()
+                sent.append(cp)
+                gacts[:, place_of] = gas[b, cols(x, tok), chunk]
+
+    work_on(in_order(0, 0), True)
+
     low = lows[x]
     for a, b in mates:
         arrived(lowr.at[a * 2 + b], r_low.at[a * 2 + b])
@@ -228,19 +345,8 @@
         cp.start()
         sent.append(cp)
 
-    order = [lax.rem(place + b, blocks) for b in range(blocks)]
-    forwards = []
-    for b in order:
-        absent = c * blocks + b != z
-        for e in range(2):
-            piece = wf.at[b, cols(y, half), pl.ds(e * feat, feat)]
-            cp = rc(piece, piece, s_f.at[b, e], r_f.at[b, e], dev(yo, z, x, c))
-            forwards.append((absent, cp))
-
-            @pl.when(absent)
-            def _():
-                arrived(piece, r_w.at[b, e])
-                cp.start()
+    for i in range(1, blocks):
+        pass_on(in_order(i, 1))
 
     for t in zs:
         arrived(upz.at[t], r_uz.at[t])
@@ -260,40 +366,13 @@
     def _():
         arrived(gdr.at[z], r_gd.at[z])
 
-    total = gdr[0]
+    total = gdr[0].astype(F32)
     for t in range(1, nz):
-        total += gdr[t]
-    gdown[...] = (total * norm).T
-
-    for i, b in enumerate(order):
-        absent = c * blocks + b != z
-
-        @pl.when(absent)
-        def _():
-            for e in range(2):
-                arrived(wf.at[b, cols(yo, half), pl.ds(e * feat, feat)], r_f.at[b, e])
-
-        @pl.when(jnp.logical_not(absent))
-        def _():
-            arrived(wf.at[b, :, cols(co, feat)], r_wl)
-
-        grad = dot(back, df[b])
-        for e in range(2):
-            part = dot(ct[:, e * feat : (e + 1) * feat], wf[b, :, e * feat : (e + 1) * feat], 1, 1)
-            grad += part.astype(BF16).astype(F32)
-        gas[i] = grad.astype(BF16)
-        block = cols(b * 2 + x, depth)
-        cp = rc(
-            gas.at[i, cols(xo, tok), :], gacts.at[:, block], s_ga.at[b], r_ga.at[b], other
-        )
-        cp.start()
-        sent.append(cp)
-        part = dot(xa[b], wf[b])
-        if i == 0:
-            vacc[...] = part
-        else:
-            vacc[...] += part
-        gacts[:, block] = gas[i, cols(x, tok), :]
+        total += gdr[t].astype(F32)
+    gdown[...] = total * norm
+
+    for i in range(1, blocks):
+        work_on(in_order(i, 0), False)
 
     vs[...] = vacc[...].astype(BF16)
     for i, (a, b) in enumerate(mates):
@@ -306,7 +385,7 @@
         )
         cp.start()
         sent.append(cp)
-    out = vacc[mine] + ADAPTER_SCALE * dot(low, up[...], 0, 0)
+    out = vacc[mine] + ADAPTER_SCALE * dot(low, uf[:, cols(c, feat)], 0, 0)
     for a, b in mates:
         arrived(vr.at[a * 2 + b], r_v.at[a * 2 + b])
         out += vr[a * 2 + b].astype(F32)
@@ -314,7 +393,10 @@
 
     arrived(gup.at[cols(xo, hr), :], r_ud)
     for b in range(blocks):
-        arrived(gacts.at[:, cols(b * 2 + xo, depth)], r_ga.at[b])
+        for h in range(2):
+            for q in range(PIECES):
+                at = cols(((b * 2 + xo) * 2 + h) * PIECES + q, rows)
+                arrived(gacts.at[:, at], r_ga.at[b, h, q])
     for cp in sent:
         cp.wait_send()
     for here, cp in gd_copies:
@@ -323,9 +405,9 @@
         def _():
             cp.wait_send()
 
-    for absent, cp in forwards:
-
-        @pl.when(absent)
+    for used, cp in own_sends + forwards:
+
+        @pl.when(used)
         def _():
             cp.wait_send()
 
@@ -355,8 +437,8 @@
         pltpu.VMEM((rank, 2 * feat), BF16),
         pltpu.VMEM((blocks, rank, depth), BF16),
         pltpu.VMEM((blocks, depth, 2 * feat), BF16),
-        pltpu.VMEM((blocks, rank, depth), F32),
-        pltpu.VMEM((nz, rank, half), F32),
+        pltpu.VMEM((blocks, rank, depth), BF16),
+        pltpu.VMEM((nz, rank, half), BF16),
         pltpu.VMEM((2, rank, tok), F32),
         pltpu.VMEM((4, rank, tok), F32),
         pltpu.VMEM((rank, feat), F32),
@@ -371,32 +453,34 @@
         dma(3), dma(4),
         dma(), dma(),
         dma(nz - 1), dma(blocks),
-        dma(nz - 1), dma(blocks, 2),
+        dma(2, PIECES), dma(blocks, 2, PIECES),
         dma(), dma(),
-        dma(blocks, 2), dma(blocks, 2),
+        dma(blocks, 2, PIECES), dma(blocks, 2, PIECES),
+        dma(blocks, 2, PIECES), dma(4 + blocks),
         dma(blocks, 2), dma(nz),
         dma(3), dma(4),
         dma(), dma(),
         dma(nz - 1), dma(nz),
         dma(), dma(),
-        dma(blocks), dma(blocks),
+        dma(blocks, 2, PIECES), dma(blocks, 2, PIECES),
         dma(3), dma(4),
     ]
-    return pl.pallas_call(
+    values, grad_acts, grad_down_t, grad_up = pl.pallas_call(
         functools.partial(exchange_kernel, nz, norm),
         out_shape=(
             jax.ShapeDtypeStruct((tok, feat), BF16),
             jax.ShapeDtypeStruct((tok, width), BF16),
-            jax.ShapeDtypeStruct((half, rank), F32),
+            jax.ShapeDtypeStruct((rank, half), F32),
             jax.ShapeDtypeStruct((rank, feat), F32),
         ),
-        in_specs=[vmem] * 5,
+        in_specs=[pl.BlockSpec(memory_space=pltpu.HBM)] * 5,
         out_specs=(vmem,) * 4,
         scratch_shapes=scratch,
         compiler_params=pltpu.CompilerParams(
             collective_id=0, has_side_effects=True, vmem_limit_bytes=48 * 2**20
         ),
     )(acts, w_value, adapt_down.T, adapter_up_factor, cotangent)
+    return values, grad_acts, grad_down_t.T, grad_up
 
 
 def body(acts, w_value, adapt_down, adapter_up_factor, cotangent):
@@ -452,7 +536,7 @@
 
 
 def pick(mesh, *arrays):
-    rows, tiles = lax.axis_size("row"), arrays[1].shape[0] % 256 == 0
+    rows, tiles = lax.axis_size("row"), arrays[1].shape[0] % (512 * PIECES // 2) == 0
     fits = rows % 4 == 0 and mesh.shape["groups"] == 2 and mesh.shape["col"] == 2
     step = kernel_body if fits and tiles else body
     return step(*arrays)

time: 111 us -> 80.2 us (0.72)
  the two profiles are of different devices: /device:TPU:25 before, /device:TPU:0 now
where the time goes in v2:
time: 80.2 us; the launch traced here: 78.9 us
  Pallas kernels  70.2 us (88%)
  local copies, waits for them, and re-layouts  8.03 us (10%)
    pallas_call x1, Pallas kernels, kernel_body(): pl.pallas_call(functools.partial(exchange_kernel, nz, norm), out_shape=(j...  70.2 us
    unnamed x14, local copies, waits for them, and re-layouts  8.03 us

profile of v2, /device:TPU:0, one launch (start us, length us, event | category | flops | bytes accessed | tf_op | source)
XLA Modules:
  0.0 78.9 jit_solution(12885101766302376879)
XLA Ops:
  0.6 0.0 copy-start
  0.6 1.2 %copy-done = bf16[128,4096]{1,0:T(8,128)(2,1)S(1)} copy-done((bf16[128,4096]{1,0:T(8,128)(2,1)S(1)}, bf16[128,4096]{1,0:T(8,128)(2,1)}, u32[]{:S(2)}) %copy-start) | copy-done | bytes 1048600
  1.9 0.0 copy-start.1
  1.9 1.2 %copy-done.1 = bf16[1024,512]{1,0:T(8,128)(2,1)S(1)} copy-done((bf16[1024,512]{1,0:T(8,128)(2,1)S(1)}, bf16[1024,512]{1,0:T(8,128)(2,1)}, u32[]{:S(2)}) %copy-start.1) | copy-done | bytes 1048600
  3.1 0.0 copy-start.2
  3.1 0.9 %copy-done.2 = bf16[1024,64]{0,1:T(8,128)(2,1)S(1)} copy-done((bf16[1024,64]{0,1:T(8,128)(2,1)S(1)}, bf16[1024,64]{0,1:T(8,128)(2,1)}, u32[]{:S(2)}) %copy-start.2) | copy-done | bytes 131096
  4.0 0.0 copy-start.3
  4.0 0.9 %copy-done.3 = bf16[128,512]{1,0:T(8,128)(2,1)S(1)} copy-done((bf16[128,512]{1,0:T(8,128)(2,1)S(1)}, bf16[128,512]{1,0:T(8,128)(2,1)}, u32[]{:S(2)}) %copy-start.3) | copy-done | bytes 131096
  4.9 0.0 copy-start.4
  4.9 0.8 %copy-done.4 = bf16[64,512]{1,0:T(8,128)(2,1)S(1)} copy-done((bf16[64,512]{1,0:T(8,128)(2,1)S(1)}, bf16[64,512]{1,0:T(8,128)(2,1)}, u32[]{:S(2)}) %copy-start.4) | copy-done | bytes 65560
  5.7 70.2 %shard_map.84 = (bf16[128,512]{1,0:T(8,128)(2,1)S(1)}, bf16[128,4096]{1,0:T(8,128)(2,1)S(1)}, f32[64,512]{1,0:T(8,128)S(1)}, f32[64,512]{1,0:T(8,128)S(1)}) custom-call(bf16[128,4096]{1,0:T(8,128)(2,1)S(1)} %copy-done, bf16[1024,512]{1,0:T(8,128)(2,1)S(1)} %copy-done.1, bf16[64,1024]{1,0:T(8,128)(2,1)S(1)} %bitcast.2, bf16[64,512]{1,0:T(8,128)(2,1)S(1)} %copy-done.4, ...), custom_call_target="tpu_custom_call" | custom-call | tf_op jit(solution)/shard_map/pallas_call | solution.py:468
  75.9 0.7 copy.13
  76.6 1.0 %copy.14 = bf16[128,4096]{1,0:T(8,128)(2,1)} copy(bf16[128,4096]{1,0:T(8,128)(2,1)S(1)} %get-tuple-element.17) | data formatting | bytes 2097152
  77.5 0.7 copy.15
  78.2 0.7 copy.16
Async XLA Ops:
  0.6 1.2 %copy-start = (bf16[128,4096]{1,0:T(8,128)(2,1)S(1)}, bf16[128,4096]{1,0:T(8,128)(2,1)}, u32[]{:S(2)}) copy-start(bf16[128,4096]{1,0:T(8,128)(2,1)} %acts.1) | copy-start | bytes 3145732
  1.9 1.2 %copy-start.1 = (bf16[1024,512]{1,0:T(8,128)(2,1)S(1)}, bf16[1024,512]{1,0:T(8,128)(2,1)}, u32[]{:S(2)}) copy-start(bf16[1024,512]{1,0:T(8,128)(2,1)} %w.1) | copy-start | bytes 3145732
  3.1 0.9 %copy-start.2 = (bf16[1024,64]{0,1:T(8,128)(2,1)S(1)}, bf16[1024,64]{0,1:T(8,128)(2,1)}, u32[]{:S(2)}) copy-start(bf16[1024,64]{0,1:T(8,128)(2,1)} %param.7) | copy-start | bytes 393220
  4.0 0.9 %copy-start.3 = (bf16[128,512]{1,0:T(8,128)(2,1)S(1)}, bf16[128,512]{1,0:T(8,128)(2,1)}, u32[]{:S(2)}) copy-start(bf16[128,512]{1,0:T(8,128)(2,1)} %cot.1) | copy-start | bytes 393220
  4.9 0.8 %copy-start.4 = (bf16[64,512]{1,0:T(8,128)(2,1)S(1)}, bf16[64,512]{1,0:T(8,128)(2,1)}, u32[]{:S(2)}) copy-start(bf16[64,512]{1,0:T(8,128)(2,1)} %up.1) | copy-start | bytes 196612

commit v3 on v2

--- a/solution.py
+++ b/solution.py
@@ -10,7 +10,7 @@
 
 ADAPTER_SCALE = 2.0
 MESH = pl.DeviceIdType.MESH
-PIECES = 2
+PIECES = 4
 F32 = jnp.float32
 BF16 = jnp.bfloat16
 
@@ -56,6 +56,9 @@
     r_up,
     s_dn,
     r_dn,
+    s_dh,
+    s_df,
+    r_df,
     s_w,
     r_w,
     s_wl,
@@ -85,6 +88,7 @@
     rank = up.shape[0]
     half, hr = depth // 2, rank // 2
     rows = half // PIECES
+    dr = rank // 2
     blocks = nz // 2
     home, place = z // blocks, z % blocks
     xo, co, yo = 1 - x, 1 - c, 1 - y
@@ -136,35 +140,38 @@
         cp.start()
         sent.append(cp)
 
-    dn_copies = [
-        rc(down_t, df.at[place], s_dn.at[k], r_dn.at[place], dev(y, t, x, c))
-        for k, t in enumerate(zs)
-    ]
-
-    @pl.when(c == home)
-    def _():
-        for cp in dn_copies:
+    w_local = rc(w, wf.at[place, :, cols(c, feat)], s_wl, r_wl, dev(y, z, x, co))
+    steps = [(i, t, (t >= 0) & (t < nz)) for i, t in enumerate((z + 1, z - 1))]
+    own_sends = []
+
+    def send_if(used, cp):
+        own_sends.append((used, cp))
+
+        @pl.when(used)
+        def _():
             cp.start()
 
-    w_local = rc(w, wf.at[place, :, cols(c, feat)], s_wl, r_wl, dev(y, z, x, co))
-
-    own_sends = []
-    for i, t in enumerate((z + 1, z - 1)):
-        there = (t >= 0) & (t < nz)
-        for q in range(PIECES):
-            piece = cols(y * PIECES + q, rows)
-            cp = rc(
-                w.at[piece, :],
-                wf.at[place, piece, cols(c, feat)],
-                s_w.at[i, q],
-                r_w.at[place, c, q],
-                dev(y, jnp.clip(t, 0, nz - 1), x, home),
+    for i, t, there in steps:
+        part = cols(y, dr)
+        to = dev(y, jnp.clip(t, 0, nz - 1), x, c)
+        send_if(
+            there & (c == home),
+            rc(down_t.at[part, :], df.at[place, part, :], s_dn.at[i], r_dn.at[place], to),
+        )
+    for q in range(PIECES):
+        for i, t, there in steps:
+            piece = cols(q * 2 + y, rows)
+            to = dev(y, jnp.clip(t, 0, nz - 1), x, home)
+            send_if(
+                there,
+                rc(
+                    w.at[piece, :],
+                    wf.at[place, piece, cols(c, feat)],
+                    s_w.at[i, q],
+                    r_w.at[place, c, q],
+                    to,
+                ),
             )
-            own_sends.append((there, cp))
-
-            @pl.when(there)
-            def _():
-                cp.start()
 
     @pl.when(c != home)
     def _():
@@ -197,40 +204,39 @@
             c == home, lax.rem(place + first + i, blocks), jnp.where(c > home, i, blocks - 1 - i)
         )
 
-    forwards = []
-
-    def pass_on(b):
+    def pass_piece(b, piece, s_next, s_side, r_here, r_side):
         source = c * blocks + b
         absent = source != z
         t = jnp.where(source < z, z + 1, z - 1)
         more = absent & (t >= 0) & (t < nz)
-        for q in range(PIECES):
-            for e in range(2):
-                piece = wf.at[b, cols(y * PIECES + q, rows), pl.ds(e * feat, feat)]
-                hop = rc(
-                    piece,
-                    piece,
-                    s_h.at[b, e, q],
-                    r_w.at[b, e, q],
-                    dev(y, jnp.clip(t, 0, nz - 1), x, c),
-                )
-                side = rc(piece, piece, s_f.at[b, e, q], r_f.at[b, e, q], dev(yo, z, x, c))
-                forwards.append((more, hop))
-                forwards.append((absent, side))
-
-                @pl.when(absent)
-                def _():
-                    arrived(piece, r_w.at[b, e, q])
-
-                @pl.when(more)
-                def _():
-                    hop.start()
-
-                @pl.when(absent)
-                def _():
-                    side.start()
-
-    pass_on(in_order(0, 1))
+
+        @pl.when(absent)
+        def _():
+            arrived(piece, r_here)
+
+        send_if(more, rc(piece, piece, s_next, r_here, dev(y, jnp.clip(t, 0, nz - 1), x, c)))
+        send_if(absent, rc(piece, piece, s_side, r_side, dev(yo, z, x, c)))
+
+    def pass_down(b):
+        piece = df.at[b, cols(y, dr), :]
+        pass_piece(b, piece, s_dh.at[b], s_df.at[b], r_dn.at[b], r_df.at[b])
+
+    def pass_on(b, q):
+        for e in range(2):
+            pass_piece(
+                b,
+                wf.at[b, cols(q * 2 + y, rows), pl.ds(e * feat, feat)],
+                s_h.at[b, e, q],
+                s_f.at[b, e, q],
+                r_w.at[b, e, q],
+                r_f.at[b, e, q],
+            )
+
+    pass_down(in_order(0, 1))
+    for q in range(PIECES):
+        pass_on(in_order(0, 1), q)
+    for i in range(1, blocks):
+        pass_down(in_order(i, 1))
 
     for cp in into:
         cp.wait()
@@ -273,7 +279,7 @@
 
         @pl.when(c * blocks + b != z)
         def _():
-            arrived(df.at[b], r_dn.at[b])
+            arrived(df.at[b, cols(yo, dr), :], r_df.at[b])
 
         low_t += dot(df[b], xa[b], 1, 1)
     lows[0] = low_t[:, :tok]
@@ -282,51 +288,62 @@
         cp = rc(lows.at[a], lowr.at[x * 2 + c], s_low.at[i], r_low.at[x * 2 + c], dev(y, z, a, b))
         cp.start()
         sent.append(cp)
-    def work_on(b, first):
+    def send_values():
+        vs[...] = vacc[...].astype(BF16)
+        for i, (a, b) in enumerate(mates):
+            cp = rc(
+                vs.at[cols(a, tok), cols(b, feat)],
+                vr.at[x * 2 + c],
+                s_v.at[i],
+                r_v.at[x * 2 + c],
+                dev(y, z, a, b),
+            )
+            cp.start()
+            sent.append(cp)
+
+    def work_on(i, q):
+        b = in_order(i, 0)
         absent = c * blocks + b != z
-
-        @pl.when(jnp.logical_not(absent))
+        chunk = pl.ds(q * 2 * rows, 2 * rows)
+        if q == 0:
+
+            @pl.when(jnp.logical_not(absent))
+            def _():
+                arrived(wf.at[b, :, cols(co, feat)], r_wl)
+
+        @pl.when(absent)
         def _():
-            arrived(wf.at[b, :, cols(co, feat)], r_wl)
-
-        for q in range(PIECES):
-            for h in (y, yo):
-                chunk = cols(h * PIECES + q, rows)
-                if h is yo:
-
-                    @pl.when(absent)
-                    def _():
-                        for e in range(2):
-                            arrived(wf.at[b, chunk, pl.ds(e * feat, feat)], r_f.at[b, e, q])
-
-                part = dot(xa[b, :, chunk], wf[b, chunk, :])
-                if first and q == 0 and h is y:
-                    vacc[...] = part
-                else:
-                    vacc[...] += part
-                grad = dot(back, df[b, :, chunk])
-                for e in range(2):
-                    part = dot(
-                        ct[:, e * feat : (e + 1) * feat],
-                        wf[b, chunk, e * feat : (e + 1) * feat],
-                        1,
-                        1,
-                    )
-                    grad += part.astype(BF16).astype(F32)
-                gas[b, :, chunk] = grad.astype(BF16)
-                place_of = cols(((b * 2 + x) * 2 + h) * PIECES + q, rows)
-                cp = rc(
-                    gas.at[b, cols(xo, tok), chunk],
-                    gacts.at[:, place_of],
-                    s_ga.at[b, h, q],
-                    r_ga.at[b, h, q],
-                    other,
-                )
-                cp.start()
-                sent.append(cp)
-                gacts[:, place_of] = gas[b, cols(x, tok), chunk]
-
-    work_on(in_order(0, 0), True)
+            for e in range(2):
+                arrived(wf.at[b, cols(q * 2 + yo, rows), pl.ds(e * feat, feat)], r_f.at[b, e, q])
+
+        part = dot(xa[b, :, chunk], wf[b, chunk, :])
+        if i == 0 and q == 0:
+            vacc[...] = part
+        else:
+            vacc[...] += part
+        if i == blocks - 1 and q == PIECES - 1:
+            send_values()
+        grad = dot(back, df[b, :, chunk])
+        for e in range(2):
+            part = dot(
+                ct[:, e * feat : (e + 1) * feat], wf[b, chunk, e * feat : (e + 1) * feat], 1, 1
+            )
+            grad += part.astype(BF16).astype(F32)
+        gas[b, :, chunk] = grad.astype(BF16)
+        at = cols((b * 2 + x) * PIECES + q, 2 * rows)
+        cp = rc(
+            gas.at[b, cols(xo, tok), chunk], gacts.at[:, at], s_ga.at[b, q], r_ga.at[b, q], other
+        )
+        cp.start()
+        sent.append(cp)
+        gacts[:, at] = gas[b, cols(x, tok), chunk]
+
+    def work_and_pass(i, q):
+        work_on(i, q)
+        if i + 1 < blocks:
+            pass_on(in_order(i + 1, 1), q)
+
+    work_and_pass(0, 0)
 
     low = lows[x]
     for a, b in mates:
@@ -338,21 +355,22 @@
     cp = rc(ups.at[cols(xo, hr), :], upx, s_ux, r_ux, other)
     cp.start()
     sent.append(cp)
+    work_and_pass(0, 1)
     arrived(upx, r_ux)
-    upz[z] = ups[cols(x, hr), :] + upx[...]
+    upz[z] = (ups[cols(x, hr), :] + upx[...]).astype(BF16)
     for k, t in enumerate(zs):
         cp = rc(upz.at[z], upz.at[z], s_uz.at[k], r_uz.at[z], dev(y, t, x, c))
         cp.start()
         sent.append(cp)
 
-    for i in range(1, blocks):
-        pass_on(in_order(i, 1))
+    for n in range(2, blocks * PIECES - 2):
+        work_and_pass(n // PIECES, n % PIECES)
 
     for t in zs:
         arrived(upz.at[t], r_uz.at[t])
-    total = upz[0]
+    total = upz[0].astype(F32)
     for t in range(1, nz):
-        total += upz[t]
+        total += upz[t].astype(F32)
     upd[...] = total * norm
     gup[cols(x, hr), :] = upd[...]
     cp = rc(upd, gup.at[cols(x, hr), :], s_ud, r_ud, other)
@@ -371,20 +389,9 @@
         total += gdr[t].astype(F32)
     gdown[...] = total * norm
 
-    for i in range(1, blocks):
-        work_on(in_order(i, 0), False)
-
-    vs[...] = vacc[...].astype(BF16)
-    for i, (a, b) in enumerate(mates):
-        cp = rc(
-            vs.at[cols(a, tok), cols(b, feat)],
-            vr.at[x * 2 + c],
-            s_v.at[i],
-            r_v.at[x * 2 + c],
-            dev(y, z, a, b),
-        )
-        cp.start()
-        sent.append(cp)
+    for n in range(blocks * PIECES - 2, blocks * PIECES):
+        work_and_pass(n // PIECES, n % PIECES)
+
     out = vacc[mine] + ADAPTER_SCALE * dot(low, uf[:, cols(c, feat)], 0, 0)
     for a, b in mates:
         arrived(vr.at[a * 2 + b], r_v.at[a * 2 + b])
@@ -393,10 +400,9 @@
 
     arrived(gup.at[cols(xo, hr), :], r_ud)
     for b in range(blocks):
-        for h in range(2):
-            for q in range(PIECES):
-                at = cols(((b * 2 + xo) * 2 + h) * PIECES + q, rows)
-                arrived(gacts.at[:, at], r_ga.at[b, h, q])
+        for q in range(PIECES):
+            at = cols((b * 2 + xo) * PIECES + q, 2 * rows)
+            arrived(gacts.at[:, at], r_ga.at[b, q])
     for cp in sent:
         cp.wait_send()
     for here, cp in gd_copies:
@@ -405,15 +411,10 @@
         def _():
             cp.wait_send()
 
-    for used, cp in own_sends + forwards:
+    for used, cp in own_sends:
 
         @pl.when(used)
         def _():
-            cp.wait_send()
-
-    @pl.when(c == home)
-    def _():
-        for cp in dn_copies:
             cp.wait_send()
 
     @pl.when(c != home)
@@ -443,7 +444,7 @@
         pltpu.VMEM((4, rank, tok), F32),
         pltpu.VMEM((rank, feat), F32),
         pltpu.VMEM((hr, feat), F32),
-        pltpu.VMEM((nz, hr, feat), F32),
+        pltpu.VMEM((nz, hr, feat), BF16),
         pltpu.VMEM((hr, feat), F32),
         pltpu.VMEM((blocks, 2 * tok, depth), BF16),
         pltpu.VMEM((2 * tok, 2 * feat), BF16),
@@ -452,7 +453,7 @@
         dma(blocks), dma(blocks),
         dma(3), dma(4),
         dma(), dma(),
-        dma(nz - 1), dma(blocks),
+        dma(2), dma(blocks), dma(blocks), dma(blocks), dma(blocks),
         dma(2, PIECES), dma(blocks, 2, PIECES),
         dma(), dma(),
         dma(blocks, 2, PIECES), dma(blocks, 2, PIECES),
@@ -462,7 +463,7 @@
         dma(), dma(),
         dma(nz - 1), dma(nz),
         dma(), dma(),
-        dma(blocks, 2, PIECES), dma(blocks, 2, PIECES),
+        dma(blocks, PIECES), dma(blocks, PIECES),
         dma(3), dma(4),
     ]
     values, grad_acts, grad_down_t, grad_up = pl.pallas_call(
@@ -477,7 +478,7 @@
         out_specs=(vmem,) * 4,
         scratch_shapes=scratch,
         compiler_params=pltpu.CompilerParams(
-            collective_id=0, has_side_effects=True, vmem_limit_bytes=48 * 2**20
+            collective_id=0, has_side_effects=True, vmem_limit_bytes=62 * 2**20
         ),
     )(acts, w_value, adapt_down.T, adapter_up_factor, cotangent)
     return values, grad_acts, grad_down_t.T, grad_up
@@ -536,7 +537,7 @@
 
 
 def pick(mesh, *arrays):
-    rows, tiles = lax.axis_size("row"), arrays[1].shape[0] % (512 * PIECES // 2) == 0
+    rows, tiles = lax.axis_size("row"), arrays[1].shape[0] % (256 * PIECES) == 0
     fits = rows % 4 == 0 and mesh.shape["groups"] == 2 and mesh.shape["col"] == 2
     step = kernel_body if fits and tiles else body
     return step(*arrays)

time: 80.2 us -> 73.6 us (0.918); the launches traced: 78.9 us -> 73.4 us
  Pallas kernels: 70.2 us -> 67.3 us
  local copies, waits for them, and re-layouts: 8.03 us -> 5.5 us
    pallas_call x1, Pallas kernels: 70.2 us -> 67.3 us  [kernel_body(): pl.pallas_call(functools.partial(exchange_kernel, nz, norm), out_shape=(j...]
    unnamed x14 -> x8, local copies, waits for them, and re-layouts: 8.03 us -> 5.5 us
where the time goes in v3:
time: 73.6 us; the launch traced here: 73.4 us
  Pallas kernels  67.3 us (91%)
  local copies, waits for them, and re-layouts  5.5 us (7%)
    pallas_call x1, Pallas kernels, kernel_body(): pl.pallas_call(functools.partial(exchange_kernel, nz, norm), out_shape=(j...  67.3 us
    unnamed x8, local copies, waits for them, and re-layouts  5.5 us

profile of v3, /device:TPU:0, one launch (start us, length us, event | category | flops | bytes accessed | tf_op | source)
XLA Modules:
  0.0 73.4 jit_solution(17506359291573405741)
XLA Ops:
  0.6 67.3 %shard_map.84 = (bf16[128,512]{1,0:T(8,128)(2,1)}, bf16[128,4096]{1,0:T(8,128)(2,1)}, f32[64,512]{1,0:T(8,128)}, f32[64,512]{1,0:T(8,128)}) custom-call(bf16[128,4096]{1,0:T(8,128)(2,1)} %acts.1, bf16[1024,512]{1,0:T(8,128)(2,1)} %w.1, bf16[64,1024]{1,0:T(8,128)(2,1)} %bitcast.2, bf16[64,512]{1,0:T(8,128)(2,1)} %up.1, bf16[128,512]{1,0:T(8,128)(2,1)} %cot.1), custom_call_target="tpu_custom_call" | custom-call | tf_op jit(solution)/shard_map/pallas_call | solution.py:469
  67.9 1.6 %copy.13 = bf16[128,512]{1,0:T(8,128)(2,1)} copy(bf16[128,512]{1,0:T(8,128)(2,1)} %get-tuple-element.16) | data formatting | bytes 262144
  69.5 0.0 copy-start.1
  69.5 2.3 %copy.14 = bf16[128,4096]{1,0:T(8,128)(2,1)} copy(bf16[128,4096]{1,0:T(8,128)(2,1)} %get-tuple-element.17) | data formatting | bytes 2097152
  71.8 0.0 copy-done.1
  71.8 0.0 copy-start
  71.8 0.7 copy.15
  72.5 0.3 copy-done
  72.7 0.7 copy.16
Async XLA Ops:
  69.5 2.3 %copy-start.1 = (f32[64,512]{1,0:T(8,128)S(1)}, f32[64,512]{1,0:T(8,128)}, u32[]{:S(2)}) copy-start(f32[64,512]{1,0:T(8,128)} %get-tuple-element.10) | copy-start | bytes 393220
  71.8 1.0 %copy-start = (f32[64,512]{1,0:T(8,128)S(1)}, f32[64,512]{1,0:T(8,128)}, u32[]{:S(2)}) copy-start(f32[64,512]{1,0:T(8,128)} %get-tuple-element.19) | copy-start | bytes 393220

commit v4 on v3

--- a/solution.py
+++ b/solution.py
@@ -264,15 +264,7 @@
                 dev(y, t, x, e),
             )
             here = (t == z) & (c == e)
-            gd_copies.append((here, cp))
-
-            @pl.when(here)
-            def _():
-                gdr[z] = gds[b, :, e * half : (e + 1) * half]
-
-            @pl.when(jnp.logical_not(here))
-            def _():
-                cp.start()
+            gd_copies.append((here, b, e, cp))
 
     low_t = jnp.zeros((rank, 2 * tok), F32)
     for b in range(blocks):
@@ -366,6 +358,16 @@
     for n in range(2, blocks * PIECES - 2):
         work_and_pass(n // PIECES, n % PIECES)
 
+    for here, b, e, cp in gd_copies:
+
+        @pl.when(here)
+        def _():
+            gdr[z] = gds[b, :, e * half : (e + 1) * half]
+
+        @pl.when(jnp.logical_not(here))
+        def _():
+            cp.start()
+
     for t in zs:
         arrived(upz.at[t], r_uz.at[t])
     total = upz[0].astype(F32)
@@ -377,18 +379,6 @@
     cp.start()
     sent.append(cp)
 
-    for t in zs:
-        arrived(gdr.at[t], r_gd.at[t])
-
-    @pl.when(c != home)
-    def _():
-        arrived(gdr.at[z], r_gd.at[z])
-
-    total = gdr[0].astype(F32)
-    for t in range(1, nz):
-        total += gdr[t].astype(F32)
-    gdown[...] = total * norm
-
     for n in range(blocks * PIECES - 2, blocks * PIECES):
         work_and_pass(n // PIECES, n % PIECES)
 
@@ -397,6 +387,18 @@
         arrived(vr.at[a * 2 + b], r_v.at[a * 2 + b])
         out += vr[a * 2 + b].astype(F32)
     values[...] = out.astype(BF16)
+
+    for t in zs:
+        arrived(gdr.at[t], r_gd.at[t])
+
+    @pl.when(c != home)
+    def _():
+        arrived(gdr.at[z], r_gd.at[z])
+
+    total = gdr[0].astype(F32)
+    for t in range(1, nz):
+        total += gdr[t].astype(F32)
+    gdown[...] = total * norm
 
     arrived(gup.at[cols(xo, hr), :], r_ud)
     for b in range(blocks):
@@ -405,7 +407,7 @@
             arrived(gacts.at[:, at], r_ga.at[b, q])
     for cp in sent:
         cp.wait_send()
-    for here, cp in gd_copies:
+    for here, _, _, cp in gd_copies:
 
         @pl.when(jnp.logical_not(here))
         def _():

time: 73.6 us -> 73.6 us (level)
  no operation moved by 1% of the time
where the time goes in v4:
time: 73.6 us; the launch traced here: 73.5 us
  Pallas kernels  67.3 us (91%)
  local copies, waits for them, and re-layouts  5.5 us (7%)
    pallas_call x1, Pallas kernels, kernel_body(): pl.pallas_call(functools.partial(exchange_kernel, nz, norm), out_shape=(j...  67.3 us
    unnamed x8, local copies, waits for them, and re-layouts  5.5 us

profile of v4, /device:TPU:0, one launch (start us, length us, event | category | flops | bytes accessed | tf_op | source)
XLA Modules:
  0.0 73.5 jit_solution(4928174378882731459)
XLA Ops:
  0.6 67.3 %shard_map.84 = (bf16[128,512]{1,0:T(8,128)(2,1)}, bf16[128,4096]{1,0:T(8,128)(2,1)}, f32[64,512]{1,0:T(8,128)}, f32[64,512]{1,0:T(8,128)}) custom-call(bf16[128,4096]{1,0:T(8,128)(2,1)} %acts.1, bf16[1024,512]{1,0:T(8,128)(2,1)} %w.1, bf16[64,1024]{1,0:T(8,128)(2,1)} %bitcast.2, bf16[64,512]{1,0:T(8,128)(2,1)} %up.1, bf16[128,512]{1,0:T(8,128)(2,1)} %cot.1), custom_call_target="tpu_custom_call" | custom-call | tf_op jit(solution)/shard_map/pallas_call | solution.py:471
  68.0 1.6 %copy.13 = bf16[128,512]{1,0:T(8,128)(2,1)} copy(bf16[128,512]{1,0:T(8,128)(2,1)} %get-tuple-element.16) | data formatting | bytes 262144
  69.5 0.0 copy-start.1
  69.5 2.3 %copy.14 = bf16[128,4096]{1,0:T(8,128)(2,1)} copy(bf16[128,4096]{1,0:T(8,128)(2,1)} %get-tuple-element.17) | data formatting | bytes 2097152
  71.8 0.0 copy-done.1
  71.8 0.0 copy-start
  71.9 0.7 copy.15
  72.5 0.3 copy-done
  72.8 0.7 copy.16
Async XLA Ops:
  69.5 2.3 %copy-start.1 = (f32[64,512]{1,0:T(8,128)S(1)}, f32[64,512]{1,0:T(8,128)}, u32[]{:S(2)}) copy-start(f32[64,512]{1,0:T(8,128)} %get-tuple-element.10) | copy-start | bytes 393220
  71.8 1.0 %copy-start = (f32[64,512]{1,0:T(8,128)S(1)}, f32[64,512]{1,0:T(8,128)}, u32[]{:S(2)}) copy-start(f32[64,512]{1,0:T(8,128)} %get-tuple-element.19) | copy-start | bytes 393220

commit v5 on v4

--- a/solution.py
+++ b/solution.py
@@ -331,9 +331,9 @@
         gacts[:, at] = gas[b, cols(x, tok), chunk]
 
     def work_and_pass(i, q):
-        work_on(i, q)
         if i + 1 < blocks:
             pass_on(in_order(i + 1, 1), q)
+        work_on(i, q)
 
     work_and_pass(0, 0)
 

time: 73.6 us -> 74.6 us (1.014)
  Pallas kernels: 67.3 us -> 68.3 us
    pallas_call x1, Pallas kernels: 67.3 us -> 68.3 us  [kernel_body(): pl.pallas_call(functools.partial(exchange_kernel, nz, norm), out_shape=(j...]
where the time goes in v5:
time: 74.6 us; the launch traced here: 74.4 us
  Pallas kernels  68.3 us (92%)
  local copies, waits for them, and re-layouts  5.5 us (7%)
    pallas_call x1, Pallas kernels, kernel_body(): pl.pallas_call(functools.partial(exchange_kernel, nz, norm), out_shape=(j...  68.3 us
    unnamed x8, local copies, waits for them, and re-layouts  5.5 us

profile of v5, /device:TPU:0, one launch (start us, length us, event | category | flops | bytes accessed | tf_op | source)
XLA Modules:
  0.0 74.4 jit_solution(6150104853170082994)
XLA Ops:
  0.6 68.3 %shard_map.84 = (bf16[128,512]{1,0:T(8,128)(2,1)}, bf16[128,4096]{1,0:T(8,128)(2,1)}, f32[64,512]{1,0:T(8,128)}, f32[64,512]{1,0:T(8,128)}) custom-call(bf16[128,4096]{1,0:T(8,128)(2,1)} %acts.1, bf16[1024,512]{1,0:T(8,128)(2,1)} %w.1, bf16[64,1024]{1,0:T(8,128)(2,1)} %bitcast.2, bf16[64,512]{1,0:T(8,128)(2,1)} %up.1, bf16[128,512]{1,0:T(8,128)(2,1)} %cot.1), custom_call_target="tpu_custom_call" | custom-call | tf_op jit(solution)/shard_map/pallas_call | solution.py:471
  68.9 1.6 %copy.13 = bf16[128,512]{1,0:T(8,128)(2,1)} copy(bf16[128,512]{1,0:T(8,128)(2,1)} %get-tuple-element.16) | data formatting | bytes 262144
  70.5 0.0 copy-start.1
  70.5 2.3 %copy.14 = bf16[128,4096]{1,0:T(8,128)(2,1)} copy(bf16[128,4096]{1,0:T(8,128)(2,1)} %get-tuple-element.17) | data formatting | bytes 2097152
  72.8 0.0 copy-done.1
  72.8 0.0 copy-start
  72.8 0.7 copy.15
  73.5 0.3 copy-done
  73.7 0.7 copy.16
Async XLA Ops:
  70.5 2.3 %copy-start.1 = (f32[64,512]{1,0:T(8,128)S(1)}, f32[64,512]{1,0:T(8,128)}, u32[]{:S(2)}) copy-start(f32[64,512]{1,0:T(8,128)} %get-tuple-element.10) | copy-start | bytes 393220
  72.8 1.0 %copy-start = (f32[64,512]{1,0:T(8,128)S(1)}, f32[64,512]{1,0:T(8,128)}, u32[]{:S(2)}) copy-start(f32[64,512]{1,0:T(8,128)} %get-tuple-element.19) | copy-start | bytes 393220
